TPU v7x, 512 devices: a whole 4x4x16 slice. The times are simulated.
512 devices in a mesh: tm: 32 (over z, core), dp: 8 (over x_lo, y), rep: 2 (over x_hi).
Axes of the slice: x: 4 (x_hi: 2, x_lo: 2; x = x_hi * 2 + x_lo), y: 4, z: 16, core: 2. Of those that a mesh axis runs over, the one named last changes fastest.
Arguments:
- clip_frames: bfloat16 [16, 128, 32, 4, 256], P(('dp', 'rep'), 'tm'), may hold values from -6 to 6
- conv_weight: bfloat16 [3, 3, 3, 256, 256], replicated, may hold values from -0.078125 to 0.078125
- up_weight: bfloat16 [256, 1024], replicated, may hold values from -0.375 to 0.375
- cotangent: bfloat16 [16, 128, 32, 4, 1024], P(('dp', 'rep'), None, 'tm'), may hold values from -6 to 6
Outputs:
- input_grad: bfloat16 [16, 128, 32, 4, 256], P(('dp', 'rep'), 'tm')
- up_grad: float32 [256, 1024], P('tm', ('dp', 'rep'))
All inputs are finite; a program needn't handle non-finite values.
Results may differ from a plain program's by a relative error of at most 0.012.
Values may be sent and summed in bfloat16 or wider, within the bound.
A program may use at most 128 MiB of HBM per device.

v0:
```python
import math
import jax
import jax.numpy as jnp
from jax import lax
from jax.sharding import PartitionSpec as P


def from_behind(value, axis, steps):
    count = lax.axis_size(axis)
    initial, last = (max(0, -steps), min(count, count - steps))
    return lax.ppermute(value, axis, [(source, source + steps) for source in range(initial, last)])


def correlate(source, kernel, frames):
    rows = source.shape[1] - 2
    cols = source.shape[2] - 2
    patches = []
    for shift_t in range(3):
        for shift_r in range(3):
            for shift_c in range(3):
                patches.append(
                    source[
                        shift_t : shift_t + frames,
                        shift_r : shift_r + rows,
                        shift_c : shift_c + cols,
                    ]
                )
    stacked = jnp.concatenate(patches, axis=-1)
    width = stacked.shape[-1]
    flat_kernel = kernel.reshape(width, kernel.shape[-1])
    return jnp.dot(stacked.reshape(-1, width), flat_kernel, preferred_element_type=jnp.float32)


def pad_space(field):
    return jnp.pad(field, ((0, 0), (1, 1), (1, 1), (0, 0)))


def local(clip_frames, conv_weight, up_weight, cotangent):
    frames_local = clip_frames[0]
    frames = frames_local.shape[0]
    rows = frames_local.shape[1]
    cols = frames_local.shape[2]
    chans = frames_local.shape[3]
    is_first = lax.axis_index("tm") == 0
    earlier = from_behind(frames_local[frames - 2 :], "tm", 1)
    earlier = jnp.where(is_first, jnp.broadcast_to(frames_local[:1], earlier.shape), earlier)
    source = pad_space(jnp.concatenate([earlier, frames_local], axis=0))
    pre = correlate(source, conv_weight, frames)
    hidden = jax.nn.silu(pre).astype(jnp.bfloat16).reshape(1, frames, rows, cols, chans)
    contract_rows = (((0,), (0,)), ((), ()))
    contract_cols = (((1,), (1,)), ((), ()))
    row_hidden = lax.all_to_all(hidden, "tm", split_axis=2, concat_axis=1, tiled=True)
    flat_h = row_hidden.reshape(-1, chans)
    flat_g = cotangent.reshape(-1, cotangent.shape[-1])
    term = lax.dot_general(flat_h, flat_g, contract_rows, preferred_element_type=jnp.float32)
    row_grad = lax.dot_general(
        flat_g, up_weight, contract_cols, preferred_element_type=jnp.float32
    ).astype(jnp.bfloat16)
    hidden_grad = lax.all_to_all(
        row_grad.reshape(row_hidden.shape), "tm", split_axis=1, concat_axis=2, tiled=True
    )
    sigma = jax.nn.sigmoid(pre)
    slope = sigma * (1.0 + pre * (1.0 - sigma))
    pre_grad = (hidden_grad.reshape(-1, chans).astype(jnp.float32) * slope).astype(jnp.bfloat16)
    pre_grad = pre_grad.reshape(frames, rows, cols, chans)
    later = from_behind(pre_grad[:2], "tm", -1)
    back_kernel = jnp.transpose(conv_weight[::-1, ::-1, ::-1], (0, 1, 2, 4, 3))
    grad_source = pad_space(jnp.concatenate([pre_grad, later], axis=0))
    input_grad = correlate(grad_source, back_kernel, frames).reshape(frames, rows, cols, chans)

    def edge_term():
        start = jnp.concatenate(
            [jnp.zeros((2, rows, cols, chans), jnp.bfloat16), pre_grad[:2]], axis=0
        )
        parts = correlate(pad_space(start), back_kernel, 2).reshape(2, rows, cols, chans)
        return parts[0] + parts[1]

    def no_term():
        return jnp.zeros((rows, cols, chans), jnp.float32)

    edge = lax.cond(is_first, edge_term, no_term)
    input_grad = input_grad.at[0].add(edge)
    time_count = lax.axis_size("tm")
    clip_count = lax.axis_size(("dp", "rep"))
    factor = 1.0 / math.sqrt(clip_count * frames * time_count * rows * cols)
    part = lax.psum_scatter(term, "tm", scatter_dimension=0, tiled=True)
    summed = lax.psum_scatter(part, ("dp", "rep"), scatter_dimension=1, tiled=True)
    return (input_grad.astype(jnp.bfloat16)[None], summed * factor)


def solution(mesh):
    in_specs = (
        P(("dp", "rep"), "tm", None, None, None),
        P(),
        P(),
        P(("dp", "rep"), None, "tm", None, None),
    )
    out_specs = (P(("dp", "rep"), "tm", None, None, None), P("tm", ("dp", "rep")))
    return jax.shard_map(local, mesh=mesh, in_specs=in_specs, out_specs=out_specs, check_vma=False)
```

profile of v0, /device:TPU:32, one launch (start us, length us, event | category | flops | bytes accessed | tf_op | source)
XLA Modules:
  0.0 382.3 jit_solution(11873751514262837852)
XLA Ops:
  8.2 1.9 collective-permute-start
  10.1 1.3 reshape.131
  12.7 16.1 %all-to-all-start = ((bf16[1,128,1,4,256]{4,3,2,0,1:T(4,128)(2,1)}), bf16[1,128,1,4,256]{4,3,2,0,1:T(4,128)(2,1)S(1)}, u32[]{:S(2)}, u32[]{:S(2)}) async-start(bf16[1,128,1,4,256]{4,3,2,0,1:T(4,128)(2,1)} %bitcast.1), calls=%async_computation | async-start | bytes 524288 | tf_op jit(solution)/shard_map/all_to_all | solution.py:59
  30.7 6.0 %copy.26 = bf16[3,3,3,256,256]{3,4,2,1,0:T(8,128)(2,1)} copy(bf16[3,3,3,256,256]{4,3,2,1,0:T(8,128)(2,1)} %param.9) | data formatting | bytes 7077888 | tf_op args[1]
  36.7 4.3 %rev.3 = bf16[3,3,3,256,256]{3,4,2,1,0:T(8,128)(2,1)} reverse(bf16[3,3,3,256,256]{3,4,2,1,0:T(8,128)(2,1)} %copy.26), dimensions={0,1,2} | reverse | bytes 7077888 | tf_op jit(solution)/shard_map/rev | solution.py:67
  41.0 4.2 %reverse_bitcast_fusion = bf16[3,3,3,256,256]{4,3,2,1,0:T(8,128)(2,1)} fusion(bf16[3,3,3,256,256]{3,4,2,1,0:T(8,128)(2,1)} %copy.26), kind=kLoop, calls=%fused_computation.175 | loop fusion | bytes 7077888 | tf_op jit(solution)/shard_map/transpose | solution.py:67
  45.5 4.1 %pad_slice_fusion.24 = (bf16[4,32,4,256]{3,2,1,0:T(4,128)(2,1)}, bf16[4,32,4,256]{3,2,1,0:T(4,128)(2,1)}, bf16[4,32,4,256]{3,2,1,0:T(4,128)(2,1)}, bf16[4,32,4,2...) fusion(bf16[6,32,4,256]{3,2,1,0:T(4,128)(2,1)S(1)} %pad_maximum, ...), kind=kLoop, calls=%fused_computation.52 | loop fusion | bytes 5373952 | tf_op jit(solution)/shard_map/slice | solution.py:22
  49.7 1.5 pad_slice_fusion.25
  51.5 1.7 concatenate.77
  54.0 1.8 concatenate.78
  55.8 1.7 concatenate.79
  58.3 1.7 concatenate.81
  60.0 1.7 concatenate.82
  61.7 1.7 concatenate.83
  63.4 1.7 concatenate.84
  65.1 1.7 concatenate.85
  66.9 1.7 concatenate.86
  68.6 1.7 concatenate.87
  70.3 1.7 concatenate.88
  72.8 1.7 concatenate.90
  74.5 1.7 concatenate.91
  76.2 1.7 concatenate.92
  77.9 1.7 concatenate.93
  79.6 1.7 concatenate.94
  81.3 1.7 concatenate.95
  86.1 1.8 constant_dynamic-update-slice_fusion.26
  87.9 1.7 constant_dynamic-update-slice_fusion.25
  89.7 1.7 constant_dynamic-update-slice_fusion.24
  91.4 1.7 constant_dynamic-update-slice_fusion.23
  93.1 1.7 constant_dynamic-update-slice_fusion.22
  94.7 1.7 constant_dynamic-update-slice_fusion.21
  96.4 1.7 constant_dynamic-update-slice_fusion.20
  98.1 1.7 constant_dynamic-update-slice_fusion.19
  99.8 1.7 constant_dynamic-update-slice_fusion.18
  101.5 1.7 constant_dynamic-update-slice_fusion.17
  103.2 1.7 constant_dynamic-update-slice_fusion.16
  104.9 1.7 constant_dynamic-update-slice_fusion.15
  106.6 1.7 constant_dynamic-update-slice_fusion.14
  108.3 1.7 constant_dynamic-update-slice_fusion.13
  119.5 6.1 %multiply_convert_fusion = (bf16[512,256]{1,0:T(8,128)(2,1)S(1)}, bf16[512,256]{1,0:T(8,128)(2,1)S(1)}) fusion(f32[512,256]{1,0:T(8,128)S(1)} %reshape.138, bf16[512,6912]{1,0:T(8,128)(2,1)} %constant_dynamic-update-slice_fusion.1, bf16[6912,256]{1,0:T(8,128)(2,1)} %bitcast.46), kind=kOutput, calls=%fused_computation.102 | convolution fusion | flops 1813381120 | bytes 11665408 | tf_op jit(solution)/shard_map/dot_general | solution.py:31
  125.7 2.0 collective-permute-start.1
  128.6 12.4 %all-to-all-start.1 = ((bf16[1,4,32,4,256]{4,3,1,0,2:T(4,128)(2,1)}), bf16[1,4,32,4,256]{4,3,1,0,2:T(4,128)(2,1)S(1)}, u32[]{:S(2)}, u32[]{:S(2)}) async-start(bf16[1,4,32,4,256]{4,3,1,0,2:T(4,128)(2,1)} %copy.28), calls=%async_computation.1 | async-start | bytes 524288 | tf_op jit(solution)/shard_map/all_to_all | solution.py:52
  156.2 5.8 %all-to-all-done.1 = bf16[1,4,32,4,256]{4,3,1,0,2:T(4,128)(2,1)S(1)} async-done(((bf16[1,4,32,4,256]{4,3,1,0,2:T(4,128)(2,1)}), bf16[1,4,32,4,256]{4,3,1,0,2:T(4,128)(2,1)S(1)}, u32[]{:S(2)}, u32[]{:S(2)}) %all-to-all-start.1) | async-done | bytes 262176 | tf_op jit(solution)/shard_map/all_to_all | solution.py:52
  162.1 1.4 fusion.53
  170.0 6.0 %fusion.52 = f32[4,32,4,256]{3,1,2,0:T(8,128)S(1)} fusion(bf16[4,32,4,6912]{3,1,2,0:T(8,128)(2,1)} %fusion.49, bf16[6912,256,1,1]{1,0,3,2:T(8,128)(2,1)} %bitcast.47), kind=kOutput, calls=%fused_computation.177 | convolution fusion | flops 1811939328 | bytes 11141120 | tf_op jit(solution)/shard_map/dot_general | solution.py:31
  176.0 109.4 %reduce-scatter.5.cloned.1.call-done = f32[8,1024]{1,0:T(8,128)} async-done(((f32[256,1024]{1,0:T(8,128)}), f32[8,1024]{1,0:T(8,128)}) %reduce-scatter.5.cloned.1.call-update) | async-done | bytes 32784 | tf_op jit(solution)/shard_map/reduce_scatter | solution.py:86
  285.4 1.8 copy.31
  288.1 86.0 %reduce-scatter.7.cloned.1.call-done = f32[64,8]{1,0:T(8,128)} async-done(((f32[1024,8]{1,0:T(8,128)}), f32[64,8]{1,0:T(8,128)}) %reduce-scatter.7.cloned.1.call-update) | async-done | bytes 2064
  (104 shorter events, 44.6 us)
Async XLA Ops:
  7.2 4.3 %copy-start = (bf16[256,1024]{1,0:T(8,128)(2,1)S(1)}, bf16[256,1024]{1,0:T(8,128)(2,1)}, u32[]{:S(2)}) copy-start(bf16[256,1024]{1,0:T(8,128)(2,1)} %param.10) | copy-start | bytes 1572868
  8.2 37.1 %collective-permute-start = (bf16[2,32,4,256]{3,2,1,0:T(4,128)(2,1)S(1)}, bf16[2,32,4,256]{3,2,1,0:T(4,128)(2,1)S(1)}, u32[]{:S(2)}, u32[]{:S(2)}) collective-permute-start(bf16[2,32,4,256]{3,2,1,0:T(4,128)(2,1)S(1)} %slice_bitcast_fusion), channel_id=1, source_target_pairs={{0,16},{16,32},{32,48},{48,64},{64,80},{80,96},{96,112},{112,128},... | collective-permute-start | bytes 393224 | tf_op jit(solution)/shard_map/ppermute | solution.py:11
  12.7 106.5 %all-to-all-start = ((bf16[1,128,1,4,256]{4,3,2,0,1:T(4,128)(2,1)}), bf16[1,128,1,4,256]{4,3,2,0,1:T(4,128)(2,1)S(1)}, u32[]{:S(2)}, u32[]{:S(2)}) async-start(bf16[1,128,1,4,256]{4,3,2,0,1:T(4,128)(2,1)} %bitcast.1), calls=%async_computation | async-start | bytes 524288 | tf_op jit(solution)/shard_map/all_to_all | solution.py:59
  36.7 8.6 %copy-start.1 = (bf16[1,4,32,4,256]{4,3,2,1,0:T(4,128)(2,1)S(1)}, bf16[1,4,32,4,256]{4,3,2,1,0:T(4,128)(2,1)}, u32[]{:S(2)}) copy-start(bf16[1,4,32,4,256]{4,3,2,1,0:T(4,128)(2,1)} %param.8) | copy-start | bytes 786436
  53.3 29.8 %copy-start.10 = (bf16[4,32,4,256]{3,2,1,0:T(4,128)(2,1)S(1)}, bf16[4,32,4,256]{3,2,1,0:T(4,128)(2,1)}, u32[]{:S(2)}) copy-start(bf16[4,32,4,256]{3,2,1,0:T(4,128)(2,1)} %get-tuple-element.51) | copy-start | bytes 786436
  54.0 29.9 %copy-start.8 = (bf16[4,32,4,256]{3,2,1,0:T(4,128)(2,1)S(1)}, bf16[4,32,4,256]{3,2,1,0:T(4,128)(2,1)}, u32[]{:S(2)}) copy-start(bf16[4,32,4,256]{3,2,1,0:T(4,128)(2,1)} %get-tuple-element.55) | copy-start | bytes 786436
  58.3 25.6 %copy-start.9 = (bf16[4,32,4,256]{3,2,1,0:T(4,128)(2,1)S(1)}, bf16[4,32,4,256]{3,2,1,0:T(4,128)(2,1)}, u32[]{:S(2)}) copy-start(bf16[4,32,4,256]{3,2,1,0:T(4,128)(2,1)} %get-tuple-element.54) | copy-start | bytes 786436
  86.1 23.9 %copy-start.7 = (bf16[512,256]{1,0:T(8,128)(2,1)S(1)}, bf16[512,256]{1,0:T(8,128)(2,1)}, u32[]{:S(2)}) copy-start(bf16[512,256]{1,0:T(8,128)(2,1)} %concatenate.91) | copy-start | bytes 786436
  86.1 24.7 %copy-start.6 = (bf16[512,256]{1,0:T(8,128)(2,1)S(1)}, bf16[512,256]{1,0:T(8,128)(2,1)}, u32[]{:S(2)}) copy-start(bf16[512,256]{1,0:T(8,128)(2,1)} %concatenate.92) | copy-start | bytes 786436
  86.1 25.4 %copy-start.5 = (bf16[512,256]{1,0:T(8,128)(2,1)S(1)}, bf16[512,256]{1,0:T(8,128)(2,1)}, u32[]{:S(2)}) copy-start(bf16[512,256]{1,0:T(8,128)(2,1)} %concatenate.93) | copy-start | bytes 786436
  86.1 26.2 %copy-start.4 = (bf16[512,256]{1,0:T(8,128)(2,1)S(1)}, bf16[512,256]{1,0:T(8,128)(2,1)}, u32[]{:S(2)}) copy-start(bf16[512,256]{1,0:T(8,128)(2,1)} %concatenate.94) | copy-start | bytes 786436
  86.1 26.9 %copy-start.3 = (bf16[512,256]{1,0:T(8,128)(2,1)S(1)}, bf16[512,256]{1,0:T(8,128)(2,1)}, u32[]{:S(2)}) copy-start(bf16[512,256]{1,0:T(8,128)(2,1)} %concatenate.95) | copy-start | bytes 786436
  86.1 27.7 %copy-start.2 = (bf16[512,256]{1,0:T(8,128)(2,1)S(1)}, bf16[512,256]{1,0:T(8,128)(2,1)}, u32[]{:S(2)}) copy-start(bf16[512,256]{1,0:T(8,128)(2,1)} %concatenate.96) | copy-start | bytes 786436
  125.7 15.6 %collective-permute-start.1 = (bf16[2,32,4,256]{3,1,2,0:T(8,128)(2,1)S(1)}, bf16[2,32,4,256]{3,1,2,0:T(8,128)(2,1)S(1)}, u32[]{:S(2)}, u32[]{:S(2)}) collective-permute-start(bf16[2,32,4,256]{3,1,2,0:T(8,128)(2,1)S(1)} %copy.23), channel_id=1, source_target_pairs={{16,0},{32,16},{48,32},{64,48},{80,64},{96,80},{112,96},{128,112},... | collective-permute-start | bytes 393224 | tf_op jit(solution)/shard_map/ppermute | solution.py:11
  128.6 33.4 %all-to-all-start.1 = ((bf16[1,4,32,4,256]{4,3,1,0,2:T(4,128)(2,1)}), bf16[1,4,32,4,256]{4,3,1,0,2:T(4,128)(2,1)S(1)}, u32[]{:S(2)}, u32[]{:S(2)}) async-start(bf16[1,4,32,4,256]{4,3,1,0,2:T(4,128)(2,1)} %copy.28), calls=%async_computation.1 | async-start | bytes 524288 | tf_op jit(solution)/shard_map/all_to_all | solution.py:52
  141.0 144.3 %reduce-scatter.5.cloned.1.call-start = ((), (), s32[]{:S(2)}) async-start(), calls=%async_computation.4 | async-start | bytes 1081344 | tf_op jit(solution)/shard_map/reduce_scatter | solution.py:86
  163.5 210.5 %reduce-scatter.7.cloned.1.call-start = ((), (), s32[]{:S(2)}) async-start(), calls=%async_computation.5 | async-start | bytes 557056
Sparse Core Ops, SparseCore 0:
  163.7 121.6 reduce-scatter.4
  288.4 85.6 reduce-scatter.6
where the time goes:
time: 384 us; the launch traced here: 382 us
  waiting for transfers between devices  201 us (52%)
  local copies, waits for them, and re-layouts  119 us (31%)
  starting transfers between devices  32.5 us (8%)
  between operations  14.4 us (4%)
  matrix products  14 us (4%)
    reduce_scatter x1, waiting for transfers between devices, local(): part = lax.psum_scatter(term, 'tm', scatter_dimension=0, tiled=True)  109 us
    unnamed x3, waiting for transfers between devices  86 us
    unnamed x79, local copies, waits for them, and re-layouts  63 us
    concatenate x29, local copies, waits for them, and re-layouts, correlate(): stacked = jnp.concatenate(patches, axis=-1)  36.3 us
    all_to_all x1, starting transfers between devices, local(): lax.all_to_all(row_grad.reshape(row_hidden.shape), 'tm', split_axis=1, co...  16.1 us
    all_to_all x1, starting transfers between devices, local(): lax.all_to_all(hidden, 'tm', split_axis=2, concat_axis=1, tiled=True)  12.4 us
    dot_general x2, matrix products, correlate(): jnp.dot(stacked.reshape(-1, width), flat_kernel, preferred_element_type=j...  12.1 us
  transfers between devices with their start and end apart: 6, of which 3 were waited for; matrix products, arithmetic and copies ran while one was open for 32% of the time, Pallas kernels for 0%

commit v1 on v0

--- a/solution.py
+++ b/solution.py
@@ -3,6 +3,7 @@
 import jax.numpy as jnp
 from jax import lax
 from jax.sharding import PartitionSpec as P
+from jax.lax import all_to_all, axis_size
 
 
 def from_behind(value, axis, steps):
@@ -49,7 +50,16 @@
     hidden = jax.nn.silu(pre).astype(jnp.bfloat16).reshape(1, frames, rows, cols, chans)
     contract_rows = (((0,), (0,)), ((), ()))
     contract_cols = (((1,), (1,)), ((), ()))
-    row_hidden = lax.all_to_all(hidden, "tm", split_axis=2, concat_axis=1, tiled=True)
+    kinds_use = lambda dim_i, ndim_at, ax_name, my_data: jnp.concatenate(
+        all_to_all(
+            jnp.stack(jnp.split(my_data, axis_size(ax_name), dim_i), 0),
+            axis_name=ax_name,
+            split_axis=0,
+            concat_axis=0,
+        ),
+        ndim_at,
+    )
+    row_hidden = kinds_use(2, 1, "tm", hidden)
     flat_h = row_hidden.reshape(-1, chans)
     flat_g = cotangent.reshape(-1, cotangent.shape[-1])
     term = lax.dot_general(flat_h, flat_g, contract_rows, preferred_element_type=jnp.float32)

time: 384 us -> 402 us (1.047)
  local copies, waits for them, and re-layouts: 119 us -> 137 us
    unnamed x79 -> x110, local copies, waits for them, and re-layouts: 63 us -> 81.7 us
    ppermute x2, waiting for transfers between devices: 0.01 us -> 9.96 us  [from_behind(): lax.ppermute(value, axis, [(source, source + steps) for source in range(i...]
    all_to_all x1, waiting for transfers between devices: 5.79 us -> 0.01 us  [local(): all_to_all(jnp.stack(jnp.split(my_data, axis_size(ax_name), dim_i), 0), a...]
    reduce_scatter x1, waiting for transfers between devices: 109 us -> 104 us  [local(): part = lax.psum_scatter(term, 'tm', scatter_dimension=0, tiled=True)]
  transfers between devices with their start and end apart: 6 -> 6, of which waited for: 3 -> 3; matrix products, arithmetic and copies ran while one was open for 32% -> 30% of each run, Pallas kernels for 0% -> 0%
where the time goes in v1:
time: 402 us; the launch traced here: 400 us
  waiting for transfers between devices  200 us (50%)
  local copies, waits for them, and re-layouts  137 us (34%)
  starting transfers between devices  32.3 us (8%)
  between operations  14.4 us (4%)
  matrix products  14 us (3%)
    reduce_scatter x1, waiting for transfers between devices, local(): part = lax.psum_scatter(term, 'tm', scatter_dimension=0, tiled=True)  104 us
    unnamed x3, waiting for transfers between devices  86 us
    unnamed x110, local copies, waits for them, and re-layouts  81.7 us
    concatenate x29, local copies, waits for them, and re-layouts, correlate(): stacked = jnp.concatenate(patches, axis=-1)  36.3 us
    all_to_all x1, starting transfers between devices, local(): lax.all_to_all(row_grad.reshape(row_hidden.shape), 'tm', split_axis=1, co...  16.1 us
    all_to_all x1, starting transfers between devices, local(): all_to_all(jnp.stack(jnp.split(my_data, axis_size(ax_name), dim_i), 0), a...  12.2 us
    dot_general x2, matrix products, correlate(): jnp.dot(stacked.reshape(-1, width), flat_kernel, preferred_element_type=j...  12.1 us
    ppermute x2, waiting for transfers between devices, from_behind(): lax.ppermute(value, axis, [(source, source + steps) for source in range(i...  9.96 us
  transfers between devices with their start and end apart: 6, of which 3 were waited for; matrix products, arithmetic and copies ran while one was open for 30% of the time, Pallas kernels for 0%

profile of v1, /device:TPU:32, one launch (start us, length us, event | category | flops | bytes accessed | tf_op | source)
XLA Modules:
  0.0 399.9 jit_solution(10126933862395973096)
XLA Ops:
  8.2 1.9 collective-permute-start
  10.1 1.3 reshape.127
  12.7 16.1 %all-to-all-start = ((bf16[1,128,1,4,256]{4,3,2,0,1:T(4,128)(2,1)}), bf16[1,128,1,4,256]{4,3,2,0,1:T(4,128)(2,1)S(1)}, u32[]{:S(2)}, u32[]{:S(2)}) async-start(bf16[1,128,1,4,256]{4,3,2,0,1:T(4,128)(2,1)} %bitcast.1), calls=%async_computation | async-start | bytes 524288 | tf_op jit(solution)/shard_map/all_to_all | solution.py:69
  30.7 6.0 %copy.49 = bf16[3,3,3,256,256]{3,4,2,1,0:T(8,128)(2,1)} copy(bf16[3,3,3,256,256]{4,3,2,1,0:T(8,128)(2,1)} %param.9) | data formatting | bytes 7077888 | tf_op args[1]
  36.7 4.3 %rev.3 = bf16[3,3,3,256,256]{3,4,2,1,0:T(8,128)(2,1)} reverse(bf16[3,3,3,256,256]{3,4,2,1,0:T(8,128)(2,1)} %copy.49), dimensions={0,1,2} | reverse | bytes 7077888 | tf_op jit(solution)/shard_map/rev | solution.py:77
  41.0 4.2 %reverse_bitcast_fusion = bf16[3,3,3,256,256]{4,3,2,1,0:T(8,128)(2,1)} fusion(bf16[3,3,3,256,256]{3,4,2,1,0:T(8,128)(2,1)} %copy.49), kind=kLoop, calls=%fused_computation.239 | loop fusion | bytes 7077888 | tf_op jit(solution)/shard_map/transpose | solution.py:77
  45.5 4.1 %pad_slice_fusion.24 = (bf16[4,32,4,256]{3,2,1,0:T(4,128)(2,1)}, bf16[4,32,4,256]{3,2,1,0:T(4,128)(2,1)}, bf16[4,32,4,256]{3,2,1,0:T(4,128)(2,1)}, bf16[4,32,4,2...) fusion(bf16[6,32,4,256]{3,2,1,0:T(4,128)(2,1)S(1)} %pad_maximum, ...), kind=kLoop, calls=%fused_computation.52 | loop fusion | bytes 5373952 | tf_op jit(solution)/shard_map/slice | solution.py:23
  49.7 1.5 pad_slice_fusion.25
  51.5 1.7 concatenate.77
  54.0 1.8 concatenate.78
  55.8 1.7 concatenate.79
  58.3 1.7 concatenate.81
  60.0 1.7 concatenate.82
  61.7 1.7 concatenate.83
  63.4 1.7 concatenate.84
  65.1 1.7 concatenate.85
  66.9 1.7 concatenate.86
  68.6 1.7 concatenate.87
  70.3 1.7 concatenate.88
  72.8 1.7 concatenate.90
  74.5 1.7 concatenate.91
  76.2 1.7 concatenate.92
  77.9 1.7 concatenate.93
  79.6 1.7 concatenate.94
  81.3 1.7 concatenate.95
  86.1 1.8 constant_dynamic-update-slice_fusion.26
  87.9 1.7 constant_dynamic-update-slice_fusion.25
  89.7 1.7 constant_dynamic-update-slice_fusion.24
  91.4 1.7 constant_dynamic-update-slice_fusion.23
  93.1 1.7 constant_dynamic-update-slice_fusion.22
  94.7 1.7 constant_dynamic-update-slice_fusion.21
  96.4 1.7 constant_dynamic-update-slice_fusion.20
  98.1 1.7 constant_dynamic-update-slice_fusion.19
  99.8 1.7 constant_dynamic-update-slice_fusion.18
  101.5 1.7 constant_dynamic-update-slice_fusion.17
  103.2 1.7 constant_dynamic-update-slice_fusion.16
  104.9 1.7 constant_dynamic-update-slice_fusion.15
  106.6 1.7 constant_dynamic-update-slice_fusion.14
  108.3 1.7 constant_dynamic-update-slice_fusion.13
  119.5 6.1 %multiply_convert_fusion = (bf16[512,256]{1,0:T(8,128)(2,1)S(1)}, bf16[512,256]{1,0:T(8,128)(2,1)S(1)}) fusion(f32[512,256]{1,0:T(8,128)S(1)} %reshape.133, bf16[512,6912]{1,0:T(8,128)(2,1)} %constant_dynamic-update-slice_fusion.1, bf16[6912,256]{1,0:T(8,128)(2,1)} %bitcast.233), kind=kOutput, calls=%fused_computation.102 | convolution fusion | flops 1813381120 | bytes 11665408 | tf_op jit(solution)/shard_map/dot_general | solution.py:32
  145.1 12.2 %all-to-all-start.1 = ((bf16[32,1,4,1,4,256]{5,4,2,3,1,0:T(4,128)(2,1)}), bf16[32,1,4,1,4,256]{5,4,2,3,1,0:T(4,128)(2,1)S(1)}, u32[]{:S(2)}, u32[]{:S(2)}) async-start(bf16[32,1,4,1,4,256]{5,4,2,3,1,0:T(4,128)(2,1)} %constant_dynamic-update-slice_fusion.29), calls=%async_computation.1 | async-start | bytes 524288 | tf_op jit(solution)/shard_map/all_to_all | solution.py:54
  157.4 2.0 collective-permute-start.1
  159.6 10.0 %collective-permute-done.1 = bf16[2,32,4,256]{3,1,2,0:T(8,128)(2,1)S(1)} collective-permute-done((bf16[2,32,4,256]{3,1,2,0:T(8,128)(2,1)S(1)}, bf16[2,32,4,256]{3,1,2,0:T(8,128)(2,1)S(1)}, u32[]{:S(2)}, u32[]{:S(2)}) %collective-permute-start.1) | collective-permute-done | bytes 131104 | tf_op jit(solution)/shard_map/ppermute | solution.py:12
  184.5 1.4 fusion.53
  192.4 6.0 %fusion.52 = f32[4,32,4,256]{3,1,2,0:T(8,128)S(1)} fusion(bf16[4,32,4,6912]{3,1,2,0:T(8,128)(2,1)} %fusion.49, bf16[6912,256,1,1]{1,0,3,2:T(8,128)(2,1)} %bitcast.234), kind=kOutput, calls=%fused_computation.241 | convolution fusion | flops 1811939328 | bytes 11141120 | tf_op jit(solution)/shard_map/dot_general | solution.py:32
  198.5 104.5 %reduce-scatter.5.cloned.1.call-done = f32[8,1024]{1,0:T(8,128)} async-done(((f32[256,1024]{1,0:T(8,128)}), f32[8,1024]{1,0:T(8,128)}) %reduce-scatter.5.cloned.1.call-update) | async-done | bytes 32784 | tf_op jit(solution)/shard_map/reduce_scatter | solution.py:96
  302.9 1.8 copy.84
  305.7 85.9 %reduce-scatter.7.cloned.1.call-done = f32[64,8]{1,0:T(8,128)} async-done(((f32[1024,8]{1,0:T(8,128)}), f32[64,8]{1,0:T(8,128)}) %reduce-scatter.7.cloned.1.call-update) | async-done | bytes 2064
  (135 shorter events, 63.1 us)
Async XLA Ops:
  7.2 4.3 %copy-start = (bf16[256,1024]{1,0:T(8,128)(2,1)S(1)}, bf16[256,1024]{1,0:T(8,128)(2,1)}, u32[]{:S(2)}) copy-start(bf16[256,1024]{1,0:T(8,128)(2,1)} %param.10) | copy-start | bytes 1572868
  8.2 37.1 %collective-permute-start = (bf16[2,32,4,256]{3,2,1,0:T(4,128)(2,1)S(1)}, bf16[2,32,4,256]{3,2,1,0:T(4,128)(2,1)S(1)}, u32[]{:S(2)}, u32[]{:S(2)}) collective-permute-start(bf16[2,32,4,256]{3,2,1,0:T(4,128)(2,1)S(1)} %slice_bitcast_fusion), channel_id=1, source_target_pairs={{0,16},{16,32},{32,48},{48,64},{64,80},{80,96},{96,112},{112,128},... | collective-permute-start | bytes 393224 | tf_op jit(solution)/shard_map/ppermute | solution.py:12
  12.7 106.5 %all-to-all-start = ((bf16[1,128,1,4,256]{4,3,2,0,1:T(4,128)(2,1)}), bf16[1,128,1,4,256]{4,3,2,0,1:T(4,128)(2,1)S(1)}, u32[]{:S(2)}, u32[]{:S(2)}) async-start(bf16[1,128,1,4,256]{4,3,2,0,1:T(4,128)(2,1)} %bitcast.1), calls=%async_computation | async-start | bytes 524288 | tf_op jit(solution)/shard_map/all_to_all | solution.py:69
  36.7 8.6 %copy-start.1 = (bf16[1,4,32,4,256]{4,3,2,1,0:T(4,128)(2,1)S(1)}, bf16[1,4,32,4,256]{4,3,2,1,0:T(4,128)(2,1)}, u32[]{:S(2)}) copy-start(bf16[1,4,32,4,256]{4,3,2,1,0:T(4,128)(2,1)} %param.8) | copy-start | bytes 786436
  53.3 29.8 %copy-start.10 = (bf16[4,32,4,256]{3,2,1,0:T(4,128)(2,1)S(1)}, bf16[4,32,4,256]{3,2,1,0:T(4,128)(2,1)}, u32[]{:S(2)}) copy-start(bf16[4,32,4,256]{3,2,1,0:T(4,128)(2,1)} %get-tuple-element.49) | copy-start | bytes 786436
  54.0 29.9 %copy-start.8 = (bf16[4,32,4,256]{3,2,1,0:T(4,128)(2,1)S(1)}, bf16[4,32,4,256]{3,2,1,0:T(4,128)(2,1)}, u32[]{:S(2)}) copy-start(bf16[4,32,4,256]{3,2,1,0:T(4,128)(2,1)} %get-tuple-element.53) | copy-start | bytes 786436
  58.3 25.6 %copy-start.9 = (bf16[4,32,4,256]{3,2,1,0:T(4,128)(2,1)S(1)}, bf16[4,32,4,256]{3,2,1,0:T(4,128)(2,1)}, u32[]{:S(2)}) copy-start(bf16[4,32,4,256]{3,2,1,0:T(4,128)(2,1)} %get-tuple-element.52) | copy-start | bytes 786436
  86.1 23.9 %copy-start.7 = (bf16[512,256]{1,0:T(8,128)(2,1)S(1)}, bf16[512,256]{1,0:T(8,128)(2,1)}, u32[]{:S(2)}) copy-start(bf16[512,256]{1,0:T(8,128)(2,1)} %concatenate.91) | copy-start | bytes 786436
  86.1 24.7 %copy-start.6 = (bf16[512,256]{1,0:T(8,128)(2,1)S(1)}, bf16[512,256]{1,0:T(8,128)(2,1)}, u32[]{:S(2)}) copy-start(bf16[512,256]{1,0:T(8,128)(2,1)} %concatenate.92) | copy-start | bytes 786436
  86.1 25.4 %copy-start.5 = (bf16[512,256]{1,0:T(8,128)(2,1)S(1)}, bf16[512,256]{1,0:T(8,128)(2,1)}, u32[]{:S(2)}) copy-start(bf16[512,256]{1,0:T(8,128)(2,1)} %concatenate.93) | copy-start | bytes 786436
  86.1 26.2 %copy-start.4 = (bf16[512,256]{1,0:T(8,128)(2,1)S(1)}, bf16[512,256]{1,0:T(8,128)(2,1)}, u32[]{:S(2)}) copy-start(bf16[512,256]{1,0:T(8,128)(2,1)} %concatenate.94) | copy-start | bytes 786436
  86.1 26.9 %copy-start.3 = (bf16[512,256]{1,0:T(8,128)(2,1)S(1)}, bf16[512,256]{1,0:T(8,128)(2,1)}, u32[]{:S(2)}) copy-start(bf16[512,256]{1,0:T(8,128)(2,1)} %concatenate.95) | copy-start | bytes 786436
  86.1 27.7 %copy-start.2 = (bf16[512,256]{1,0:T(8,128)(2,1)S(1)}, bf16[512,256]{1,0:T(8,128)(2,1)}, u32[]{:S(2)}) copy-start(bf16[512,256]{1,0:T(8,128)(2,1)} %concatenate.96) | copy-start | bytes 786436
  145.1 39.4 %all-to-all-start.1 = ((bf16[32,1,4,1,4,256]{5,4,2,3,1,0:T(4,128)(2,1)}), bf16[32,1,4,1,4,256]{5,4,2,3,1,0:T(4,128)(2,1)S(1)}, u32[]{:S(2)}, u32[]{:S(2)}) async-start(bf16[32,1,4,1,4,256]{5,4,2,3,1,0:T(4,128)(2,1)} %constant_dynamic-update-slice_fusion.29), calls=%async_computation.1 | async-start | bytes 524288 | tf_op jit(solution)/shard_map/all_to_all | solution.py:54
  157.2 145.7 %reduce-scatter.5.cloned.1.call-start = ((), (), s32[]{:S(2)}) async-start(), calls=%async_computation.4 | async-start | bytes 1081344 | tf_op jit(solution)/shard_map/reduce_scatter | solution.py:96
  157.4 12.2 %collective-permute-start.1 = (bf16[2,32,4,256]{3,1,2,0:T(8,128)(2,1)S(1)}, bf16[2,32,4,256]{3,1,2,0:T(8,128)(2,1)S(1)}, u32[]{:S(2)}, u32[]{:S(2)}) collective-permute-start(bf16[2,32,4,256]{3,1,2,0:T(8,128)(2,1)S(1)} %copy.46), channel_id=1, source_target_pairs={{16,0},{32,16},{48,32},{64,48},{80,64},{96,80},{112,96},{128,112},... | collective-permute-start | bytes 393224 | tf_op jit(solution)/shard_map/ppermute | solution.py:12
  186.0 205.6 %reduce-scatter.7.cloned.1.call-start = ((), (), s32[]{:S(2)}) async-start(), calls=%async_computation.5 | async-start | bytes 557056
Sparse Core Ops, SparseCore 0:
  186.1 116.7 reduce-scatter.4
  305.9 85.6 reduce-scatter.6
